TPU v7x, 256 devices: a whole 4x4x8 slice. The times are simulated.
256 devices in a mesh: lat: 16 (over x_hi, y, core), lon: 16 (over z, x_lo).
Axes of the slice: x: 4 (x_hi: 2, x_lo: 2; x = x_hi * 2 + x_lo), y: 4, z: 8, core: 2. Of those that a mesh axis runs over, the one named last changes fastest.
Arguments:
- fine_tokens: bfloat16 [384, 768, 512], P('lat', 'lon'), may hold values from -6 to 6
- merge_gain: float32 [2048], replicated, may hold values from 0.25 to 1.75
- merge_weight: bfloat16 [2048, 1024], P('lat'), may hold values from -0.125 to 0.125
- attn_gain: float32 [1024], replicated, may hold values from 0.25 to 1.75
- qkv_weight: bfloat16 [1024, 3072], P('lat'), may hold values from -0.1875 to 0.1875
- proj_weight: bfloat16 [1024, 1024], P('lat'), may hold values from -0.1875 to 0.1875
- bias_table: float32 [16, 529], replicated, may hold values from -3 to 300, as said below
- region_ids: int32 [192, 384], P('lat', 'lon'), may hold values from 0 to 3
- row_counts: int32 [16], replicated, may hold values from 1 to 12, 144 in all
- cotangent: bfloat16 [192, 384, 1024], P('lat', 'lon'), may hold values from -6 to 6
Outputs:
- output: bfloat16 [192, 384, 1024], P('lat', 'lon')
- grad_fine: bfloat16 [384, 768, 512], P('lat', 'lon')
Inputs may be any that keep to these rules, and one draw needn't show every extreme that they name: row_counts[i] live rows are the first slots of latitude device i. `bias_table`: bias of each head for each relative offset.
All inputs are finite; a program needn't handle non-finite values.
Results may differ from a plain program's by a relative error of at most 0.015.
Values may be sent and summed in bfloat16 or wider, within the bound.
A program may use at most 192 MiB of HBM per device.

v0:
```python
import functools

import jax
import jax.numpy as jnp
from jax import lax
from jax.experimental import pallas as pl
from jax.experimental.pallas import tpu as pltpu
from jax.sharding import PartitionSpec as P

MESH = pl.DeviceIdType.MESH
BF16 = jnp.bfloat16
F32 = jnp.float32
NORM_EPS = 1e-05
MASKED = -1000000000.0
NT = (((1,), (1,)), ((), ()))
TN = (((0,), (0,)), ((), ()))

KEYS = [(1, 0), (0, 3), (0, 1), (0, 2), (1, 3), (1, 1), (1, 2)]
CROSS = [(1, 0), (0, 3), (0, 1), (0, 2, 0), (0, 2, 1), (1, 3), (1, 1), (1, 2)]
RID = {("c",) + k: i for i, k in enumerate(CROSS)}
RID.update({("r",) + k: 8 + i for i, k in enumerate(KEYS)})
RID.update({("k",) + k: 15 + i for i, k in enumerate(KEYS)})
RID.update({("q",) + k: 22 + i for i, k in enumerate(KEYS)})
RID[("own",)] = 29
N_IDS = 30
LINK = {
    (1, 0): "zp",
    (0, 3): "zm",
    (0, 1): "xl",
    (0, 2): "zp",
    (1, 3): "xl",
    (1, 1): "zm",
    (1, 2): "zp",
}

TC, TL, BR, BL, BLX = 0, 1, 2, 3, 4
SLOT = ((0, 80), (80, 48), (128, 48), (176, 48), (224, 48))
IN_ROWS, OUT_ROWS = 272, 224


class Gather:
    def __init__(self, shards, fulls, send_sem, recv_sem, local_sem):
        self.shards, self.fulls = shards, fulls
        self.send_sem, self.recv_sem, self.local_sem = send_sem, recv_sem, local_sem
        lat, lon = lax.axis_index("lat"), lax.axis_index("lon")
        a, y, k = lat // 8, (lat // 2) % 4, lat % 2
        z, xlo = lon // 2, lon % 2
        self.a, self.y, self.k = a, y, k
        self.c = (xlo + a + z) % 2

        def at(a_, y_, k_):
            return a_ * 8 + y_ * 2 + k_

        self.near = dict(
            yp=(at(a, (y + 1) % 4, k), lon),
            ym=(at(a, (y + 3) % 4, k), lon),
            xh=(at(1 - a, y, k), z * 2 + (1 - xlo)),
            xl=(lat, z * 2 + (1 - xlo)),
            zp=(lat, ((z + 1) % 8) * 2 + xlo),
            zm=(lat, ((z + 7) % 8) * 2 + xlo),
            core=(at(a, y, 1 - k), lon),
        )
        self.sent, self.local = [], []
        self.count = [0] * len(shards)

    def rows(self, w, key, half, core):
        r = self.shards[w].shape[0]
        a = self.a if key[0] == 0 else 1 - self.a
        s = a * 8 + ((self.y + key[1]) % 4) * 2 + core
        if half is None:
            return pl.ds(pl.multiple_of(s * r, r), r)
        off, n = half * (r // 2), r // 2
        if len(key) == 3:
            off, n = off + key[2] * (r // 4), r // 4
        return pl.ds(pl.multiple_of(s * r + off, n), n)

    def copy(self, w, rid, src, dst, dev, i):
        return pltpu.make_async_remote_copy(
            src_ref=src,
            dst_ref=dst,
            send_sem=self.send_sem.at[w, i],
            recv_sem=self.recv_sem.at[w, RID[rid]],
            device_id=dev,
            device_id_type=MESH,
        )

    def send(self, w, where, to, rid, src=None):
        full = self.fulls[w]
        i = self.count[w]
        self.count[w] += 1
        src = full.at[where] if src is None else src
        cp = self.copy(w, rid, src, full.at[where], self.near[to], i)
        cp.start()
        self.sent.append(cp)

    def recv(self, w, rid, where):
        part = self.fulls[w].at[where]
        self.copy(w, rid, part, part, self.near["core"], 0).wait_recv()

    def s0(self, w):
        shard = self.shards[w]
        r = shard.shape[0]
        where = self.rows(w, (0, 0), self.c, self.k)
        half = shard.at[pl.ds(pl.multiple_of(self.c * (r // 2), r // 2), r // 2)]
        self.send(w, where, "xh", ("c", 1, 0), half)
        self.send(w, where, "yp", ("c", 0, 3), half)
        self.send(w, where, "ym", ("c", 0, 1), half)
        whole = self.rows(w, (0, 0), None, self.k)
        self.send(w, whole, "core", ("own",), shard)
        cp = pltpu.make_async_copy(shard, self.fulls[w].at[whole], self.local_sem.at[w])
        cp.start()
        self.local.append(cp)

    def spread(self, w, key):
        where = self.rows(w, key, self.c, self.k)
        self.send(w, where, LINK[key], ("r",) + key)
        self.send(w, where, "core", ("k",) + key)

    def s1(self, w):
        c, k = self.c, self.k
        where = self.rows(w, (1, 0), c, k)
        self.recv(w, ("c", 1, 0), where)
        self.send(w, where, "yp", ("c", 1, 3))
        self.send(w, where, "ym", ("c", 1, 1))
        self.spread(w, (1, 0))
        self.recv(w, ("c", 0, 3), self.rows(w, (0, 3), c, k))
        self.send(w, self.rows(w, (0, 3, 0), c, k), "yp", ("c", 0, 2, 0))
        self.spread(w, (0, 3))
        self.recv(w, ("c", 0, 1), self.rows(w, (0, 1), c, k))
        self.send(w, self.rows(w, (0, 1, 1), c, k), "ym", ("c", 0, 2, 1))
        self.spread(w, (0, 1))

    def s2(self, w):
        c, k = self.c, self.k
        self.recv(w, ("c", 0, 2, 0), self.rows(w, (0, 2, 0), c, k))
        self.recv(w, ("c", 0, 2, 1), self.rows(w, (0, 2, 1), c, k))
        self.send(w, self.rows(w, (0, 2), c, k), "xh", ("c", 1, 2))
        self.spread(w, (0, 2))

    def s3(self, w):
        for key in ((1, 3), (1, 1), (1, 2)):
            self.recv(w, ("c",) + key, self.rows(w, key, self.c, self.k))
            self.spread(w, key)

    def s4(self, w):
        for key in KEYS:
            where = self.rows(w, key, 1 - self.c, self.k)
            self.recv(w, ("r",) + key, where)
            self.send(w, where, "core", ("q",) + key)

    def fin(self, w):
        self.recv(w, ("own",), self.rows(w, (0, 0), None, 1 - self.k))
        for key in KEYS:
            self.recv(w, ("k",) + key, self.rows(w, key, self.c, 1 - self.k))
            self.recv(w, ("q",) + key, self.rows(w, key, 1 - self.c, 1 - self.k))
        self.local[w].wait()

    def drain(self):
        for cp in self.sent:
            cp.wait_send()


def over12(v):
    return (v * 171) >> 11


def over6(v):
    return (v * 171) >> 10


def window_source(d, lat):
    second = d >= 144
    e = jnp.where(second, d - 144, d)
    r = over12(e)
    c = e - 12 * r
    none = jnp.full(d.shape, -1, jnp.int32)
    lats = jnp.zeros(d.shape, jnp.int32) + lat
    upper = r < 6
    left = c < 6
    edge = (r - 6) * 6 + (c - 6)
    last = lats == 15
    first = lats == 0
    own_a = jnp.where(upper, (6 + r) * 24 + 6 + c, jnp.where(last & left, r * 24 + 18 + c, none))
    in_a = jnp.where(
        upper,
        none,
        jnp.where(last, jnp.where(left, none, SLOT[BLX][0] + edge), (r - 6) * 12 + c),
    )
    own_b = jnp.where(
        upper,
        jnp.where(first, r * 24 + 6 + c, none),
        jnp.where(left, (r - 6) * 24 + 18 + c, none),
    )
    in_top = jnp.where(left, SLOT[BR][0] + r * 6 + c, SLOT[BL][0] + r * 6 + c - 6)
    in_b = jnp.where(
        upper,
        jnp.where(first, none, in_top),
        jnp.where(left, none, SLOT[TL][0] + edge),
    )
    return jnp.where(second, own_b, own_a), jnp.where(second, in_b, in_a)


def slot_source(s):
    none = jnp.full(s.shape, -1, jnp.int32)
    r12 = over12(s)
    tc = jnp.where(s < 72, r12 * 24 + 6 + s - 12 * r12, none)

    def corner(base, row, col):
        t = s - base
        r = over6(t)
        return jnp.where(t < 36, (row + r) * 24 + col + t - 6 * r, none)

    tl, br, bl = corner(80, 0, 0), corner(128, 6, 18), corner(176, 6, 0)
    return jnp.where(s < 80, tc, jnp.where(s < 128, tl, jnp.where(s < 176, br, bl)))


def column(n):
    return lax.broadcasted_iota(jnp.int32, (n, 1), 0)


def line(n):
    return lax.broadcasted_iota(jnp.int32, (1, n), 1)


def pick(source, rows, cols):
    axis = 1 if source.shape[1] == 1 else 0
    place = lax.broadcasted_iota(jnp.int32, (rows, cols), axis)
    return (source == place).astype(F32).astype(BF16)


def dot(a, b):
    return jnp.dot(a, b, preferred_element_type=F32)


def dot_nt(a, b):
    return lax.dot_general(a, b, NT, preferred_element_type=F32)


def dot_tn(a, b):
    return lax.dot_general(a, b, TN, preferred_element_type=F32)


def norm_rows(v):
    n = v.shape[-1]
    centred = v - jnp.sum(v, axis=-1, keepdims=True) * (1.0 / n)
    inv = lax.rsqrt(jnp.sum(centred * centred, axis=-1, keepdims=True) * (1.0 / n) + NORM_EPS)
    return centred * inv, inv


def kernel(
    fine,
    merge_gain,
    merge_shard,
    attn_gain,
    qkv_shard,
    proj_shard,
    table,
    region,
    counts,
    cot,
    out,
    grad_fine,
    merge,
    qkv_w,
    proj,
    g_send,
    g_recv,
    g_local,
    f_send,
    f_recv,
    b_send,
    b_recv,
    out_cot,
    out_mer,
    in_cot,
    in_mer,
    back_out,
    back_grad,
    home_out,
    home_grad,
    patch_n,
    merged_home,
    win_mer,
    win_cot,
    normed,
    proj_all,
    upstream,
    attended,
    grad_all,
    wide,
    grad_patch,
    lines,
    split,
    bias,
    mask,
    tag_pad,
):
    lat, lon = lax.axis_index("lat"), lax.axis_index("lon")
    up = ((lat + 15) % 16, lon)
    down = ((lat + 1) % 16, lon)
    left = (lat, (lon + 15) % 16)
    right = (lat, (lon + 1) % 16)
    down_left = ((lat + 1) % 16, (lon + 15) % 16)
    up_right = ((lat + 15) % 16, (lon + 1) % 16)
    gather = Gather((merge_shard, qkv_shard, proj_shard), (merge, qkv_w, proj), g_send, g_recv, g_local)

    for ref in (in_cot, in_mer, home_out, home_grad):
        ref[...] = jnp.zeros_like(ref)
    barrier = pltpu.get_barrier_semaphore()
    partners = list(gather.near.values()) + [up, down, left, right, down_left, up_right]
    for dev in partners:
        pl.semaphore_signal(barrier, inc=1, device_id=dev, device_id_type=MESH)
    pl.semaphore_wait(barrier, len(partners))

    not_first, not_last, is_last = lat > 0, lat < 15, lat == 15

    def forward(m, src, dst, do):
        def go(slot_from, slot_to, dev):
            f0, n = SLOT[slot_from]
            t0 = SLOT[slot_to][0]
            do(
                pltpu.make_async_remote_copy(
                    src_ref=src.at[pl.ds(f0, n)],
                    dst_ref=dst.at[pl.ds(t0, n)],
                    send_sem=f_send.at[m, slot_from],
                    recv_sem=f_recv.at[m, slot_to],
                    device_id=dev,
                    device_id_type=MESH,
                )
            )

        go(TL, TL, left)

        @pl.when(not_first)
        def _():
            go(TC, TC, up)

        @pl.when(not_last)
        def _():
            go(BR, BR, down)
            go(BL, BL, down_left)

        @pl.when(is_last)
        def _():
            go(BL, BLX, left)

    def forward_recv(m, dst):
        def got(slot):
            f0, n = SLOT[slot]
            part = dst.at[pl.ds(f0, n)]
            pltpu.make_async_remote_copy(
                src_ref=part,
                dst_ref=part,
                send_sem=f_send.at[m, 0],
                recv_sem=f_recv.at[m, slot],
                device_id=right,
                device_id_type=MESH,
            ).wait_recv()

        got(TL)

        @pl.when(not_last)
        def _():
            got(TC)

        @pl.when(not_first)
        def _():
            got(BR)
            got(BL)

        @pl.when(is_last)
        def _():
            got(BLX)

    def backward(m, src, dst, do):
        def go(slot_from, slot_to, dev):
            f0, n = SLOT[slot_from]
            t0 = SLOT[slot_to][0]
            do(
                pltpu.make_async_remote_copy(
                    src_ref=src.at[pl.ds(f0, n)],
                    dst_ref=dst.at[pl.ds(t0, n)],
                    send_sem=b_send.at[m, slot_from],
                    recv_sem=b_recv.at[m, slot_to],
                    device_id=dev,
                    device_id_type=MESH,
                )
            )

        go(TL, TL, right)

        @pl.when(not_last)
        def _():
            go(TC, TC, down)

        @pl.when(not_first)
        def _():
            go(BR, BR, up)
            go(BL, BL, up_right)

        @pl.when(is_last)
        def _():
            go(BLX, BL, right)

    def backward_recv(m, dst):
        def got(slot):
            f0, n = SLOT[slot]
            part = dst.at[pl.ds(f0, n)]
            pltpu.make_async_remote_copy(
                src_ref=part,
                dst_ref=part,
                send_sem=b_send.at[m, 0],
                recv_sem=b_recv.at[m, slot],
                device_id=right,
                device_id_type=MESH,
            ).wait_recv()

        got(TL)
        got(BL)

        @pl.when(not_first)
        def _():
            got(TC)

        @pl.when(not_last)
        def _():
            got(BR)

    def start(cp):
        cp.start()

    def sent(cp):
        cp.wait_send()

    gather.s0(0)
    tag_pad[...] = jnp.zeros_like(tag_pad)
    tag_pad[0:12, 0:24] = (region[...] + 1).astype(F32)
    cell = column(288)
    cell_row = (cell * 171) >> 12
    cell_col = cell - 24 * cell_row
    row_pick = (cell_row == lax.broadcasted_iota(jnp.int32, (288, 16), 1)).astype(F32).astype(BF16)
    tags = dot(row_pick, tag_pad[...].astype(BF16))
    lanes128 = lax.broadcasted_iota(jnp.int32, (288, 128), 1)
    tag = jnp.sum(jnp.where(lanes128 == cell_col, tags, 0.0), axis=-1, keepdims=True)
    tag = tag * (cell_row < counts[lat]).astype(F32)
    tag_home = jnp.broadcast_to(tag, (288, 128)).astype(BF16)
    to_slots = pick(slot_source(column(OUT_ROWS)), OUT_ROWS, 288)
    out_cot[:, 0:1024] = dot(to_slots, cot[...]).astype(BF16)
    out_cot[:, 1024:1152] = dot(to_slots, tag_home).astype(BF16)
    forward(0, out_cot, in_cot, start)

    o = column(192)
    block = jnp.where(o < 48, 0, jnp.where(o < 96, 1, jnp.where(o < 144, 2, 3)))
    within = o - 48 * block
    wr = (within >= 24).astype(jnp.int32)
    wc = within - 24 * wr
    to_blocks = pick((2 * wr + (block & 1)) * 48 + 2 * wc + (block >> 1), 192, 192)

    def patch_stats(g):
        raw = dot(to_blocks, fine[pl.ds(pl.multiple_of(g * 192, 192), 192), :])
        parts = [raw[48 * b : 48 * b + 48] for b in range(4)]
        average = sum(jnp.sum(p, axis=-1, keepdims=True) for p in parts) * (1.0 / 2048)
        parts = [p - average for p in parts]
        spread = sum(jnp.sum(p * p, axis=-1, keepdims=True) for p in parts) * (1.0 / 2048)
        inv = lax.rsqrt(spread + NORM_EPS)
        return [p * inv for p in parts], inv

    def patches(g, _):
        parts, _inv = patch_stats(g)
        at = pl.ds(pl.multiple_of(g * 48, 48), 48)
        for b in range(4):
            gain = merge_gain[:, 512 * b : 512 * b + 512]
            patch_n[at, 512 * b : 512 * b + 512] = (parts[b] * gain).astype(BF16)
        return 0

    def bias_lines(c, _):
        lane = line(384)
        u = over12(lane)
        index = jnp.where(lane < 276, u * 23 + (lane - 12 * u) - c + 11, -1)
        three = dot(split[...], pick(index, 640, 384))
        lines[c] = three[0:16] + three[16:32] + three[32:48]
        return 0

    gather.s1(0)
    gather.s0(1)
    lax.fori_loop(0, 3, patches, 0)
    gather.s2(0)
    lax.fori_loop(3, 6, patches, 0)
    gather.s3(0)
    gather.s1(1)
    gather.s0(2)
    t = table[...]
    high = t.astype(BF16)
    rest = t - high.astype(F32)
    middle = rest.astype(BF16)
    split[...] = jnp.zeros_like(split)
    split[0:16, 0:529] = high
    split[16:32, 0:529] = middle
    split[32:48, 0:529] = (rest - middle.astype(F32)).astype(BF16)
    lax.fori_loop(0, 6, bias_lines, 0)
    gather.s4(0)
    gather.s2(1)
    lax.fori_loop(6, 12, bias_lines, 0)
    gather.fin(0)

    def merge_tile(n, _):
        at = pl.ds(pl.multiple_of(n * 256, 256), 256)
        merged_home[:, at] = dot(patch_n[...], merge[:, at]).astype(BF16)
        return 0

    lax.fori_loop(0, 4, merge_tile, 0)
    out_mer[...] = dot(to_slots, merged_home[...]).astype(BF16)
    forward(1, out_mer, in_mer, start)

    gather.s3(1)
    gather.s1(2)
    for h in range(16):
        some = lines[:, h, :]
        for r in range(12):
            bias[h, 12 * r : 12 * r + 12, :] = some[:, 12 * (11 - r) : 12 * (11 - r) + 144]
    gather.s4(1)
    gather.s2(2)

    own, came = window_source(column(288), lat)
    from_home = pick(own, 288, 288)
    from_slots = pick(came, 288, IN_ROWS)
    forward_recv(0, in_cot)
    win_cot[...] = (dot(from_home, cot[...]) + dot(from_slots, in_cot[:, 0:1024])).astype(BF16)
    win_tag = dot(from_home, tag_home) + dot(from_slots, in_cot[:, 1024:1152])
    d = lax.broadcasted_iota(jnp.int32, (288, 128), 0)
    apart = ((lat == 15) & (d >= 72) & (d < 144)) | ((lat == 0) & (d >= 144) & (d < 216))
    live = (win_tag > 0).astype(F32)
    win_tag = win_tag + 8.0 * live * apart.astype(F32)
    for w in range(2):
        at = slice(144 * w, 144 * w + 144)
        key_tag = win_tag[at, 0:1]
        query_tag = jnp.transpose(win_tag[at])[0:1]
        allowed = (key_tag == query_tag) & (key_tag > 0)
        mask[w] = jnp.where(allowed, 0.0, MASKED)
    gather.s3(2)
    gather.s4(2)
    forward_recv(1, in_mer)
    win_mer[...] = (dot(from_home, merged_home[...]) + dot(from_slots, in_mer[...])).astype(BF16)

    def norm_chunk(g, _):
        at = pl.ds(pl.multiple_of(g * 48, 48), 48)
        normed[at, :] = (norm_rows(win_mer[at, :].astype(F32))[0] * attn_gain[...]).astype(BF16)
        return 0

    lax.fori_loop(0, 6, norm_chunk, 0)
    gather.fin(1)

    def qkv_tile(n, _):
        at = pl.ds(pl.multiple_of(n * 256, 256), 256)
        proj_all[:, at] = dot(normed[...], qkv_w[:, at]).astype(BF16)
        return 0

    lax.fori_loop(0, 12, qkv_tile, 0)
    gather.fin(2)
    live_col = live[:, 0:1]

    def upstream_tile(n, _):
        at = pl.ds(pl.multiple_of(n * 256, 256), 256)
        upstream[:, at] = (dot_nt(win_cot[...], proj[at, :]) * live_col).astype(BF16)
        return 0

    lax.fori_loop(0, 4, upstream_tile, 0)

    lane = lax.broadcasted_iota(jnp.int32, (144, 128), 1)

    def attend(pair, _):
        off = pl.multiple_of(pair * 128, 128)
        for w in range(2):
            rows = pl.ds(144 * w, 144)
            q = proj_all[rows, pl.ds(off, 128)] * jnp.asarray(0.125, BF16)
            k = proj_all[rows, pl.ds(1024 + off, 128)]
            v = proj_all[rows, pl.ds(2048 + off, 128)]
            u = upstream[rows, pl.ds(off, 128)]
            sums = [0.0, 0.0, 0.0, 0.0]
            for e in range(2):
                half = (lane < 64) if e == 0 else (lane >= 64)
                qe, ke, ve, ue = [jnp.where(half, x, jnp.zeros_like(x)) for x in (q, k, v, u)]
                scores = dot_nt(ke, q) + bias[2 * pair + e] + mask[w]
                powers = jnp.exp(scores - jnp.max(scores, axis=0, keepdims=True))
                probs = powers * (1.0 / jnp.sum(powers, axis=0, keepdims=True))
                low = probs.astype(BF16)
                grads = dot_nt(ve, u)
                rows_dot = jnp.sum(probs * grads, axis=0, keepdims=True)
                logits = (probs * (grads - rows_dot)).astype(BF16)
                terms = (dot_tn(low, ve), dot_tn(logits, ke), dot(logits, qe), dot(low, ue))
                sums = [s + x for s, x in zip(sums, terms)]
            alive = live[144 * w : 144 * w + 144]
            attended[rows, pl.ds(off, 128)] = (sums[0] * alive).astype(BF16)
            grad_all[rows, pl.ds(off, 128)] = (sums[1] * 0.125).astype(BF16)
            grad_all[rows, pl.ds(1024 + off, 128)] = sums[2].astype(BF16)
            grad_all[rows, pl.ds(2048 + off, 128)] = sums[3].astype(BF16)
        return 0

    lax.fori_loop(0, 8, attend, 0)

    def out_tile(n, _):
        at = pl.ds(pl.multiple_of(n * 256, 256), 256)
        total = win_mer[:, at].astype(F32) + dot(attended[...], proj[:, at])
        normed[:, at] = total.astype(BF16)
        return 0

    lax.fori_loop(0, 4, out_tile, 0)
    own_l, came_l = window_source(line(288), lat)
    to_in_slots = pick(came_l, IN_ROWS, 288)
    to_home = pick(own_l, 288, 288)
    slots_home = pick(slot_source(line(OUT_ROWS)), 288, OUT_ROWS)
    back_out[...] = dot(to_in_slots, normed[...]).astype(BF16)
    backward(0, back_out, home_out, start)

    def grad_tile(n, _):
        at = pl.ds(pl.multiple_of(n * 256, 256), 256)
        wide[:, at] = dot_nt(grad_all[...], qkv_w[at, :])
        return 0

    lax.fori_loop(0, 4, grad_tile, 0)

    def norm_back_chunk(g, _):
        at = pl.ds(pl.multiple_of(g * 48, 48), 48)
        n, inv = norm_rows(win_mer[at, :].astype(F32))
        weighted = wide[at, :] * attn_gain[...]
        first = jnp.sum(weighted, axis=-1, keepdims=True) * (1.0 / 1024)
        second = jnp.sum(weighted * n, axis=-1, keepdims=True) * (1.0 / 1024)
        back = win_cot[at, :].astype(F32) + inv * (weighted - first - n * second)
        win_cot[at, :] = back.astype(BF16)
        return 0

    lax.fori_loop(0, 6, norm_back_chunk, 0)
    back_grad[...] = dot(to_in_slots, win_cot[...]).astype(BF16)
    backward(1, back_grad, home_grad, start)
    backward_recv(0, home_out)
    out[...] = (dot(to_home, normed[...]) + dot(slots_home, home_out[...])).astype(BF16)
    backward_recv(1, home_grad)
    merged_home[...] = (dot(to_home, win_cot[...]) + dot(slots_home, home_grad[...])).astype(BF16)

    def patch_tile(n, _):
        at = pl.ds(pl.multiple_of(n * 256, 256), 256)
        grad_patch[:, at] = dot_nt(merged_home[...], merge[at, :])
        return 0

    lax.fori_loop(0, 8, patch_tile, 0)

    def patch_back(g, _):
        parts, inv = patch_stats(g)
        at = pl.ds(pl.multiple_of(g * 48, 48), 48)
        weighted = [
            grad_patch[at, 512 * b : 512 * b + 512] * merge_gain[:, 512 * b : 512 * b + 512]
            for b in range(4)
        ]
        first = sum(jnp.sum(x, axis=-1, keepdims=True) for x in weighted) * (1.0 / 2048)
        second = sum(
            jnp.sum(x * n, axis=-1, keepdims=True) for x, n in zip(weighted, parts)
        ) * (1.0 / 2048)
        back = [(inv * (x - first - n * second)).astype(BF16) for x, n in zip(weighted, parts)]
        tokens = dot_tn(to_blocks, jnp.concatenate(back, axis=0))
        grad_fine[pl.ds(pl.multiple_of(g * 192, 192), 192), :] = tokens.astype(BF16)
        return 0

    lax.fori_loop(0, 6, patch_back, 0)

    gather.drain()
    forward(0, out_cot, in_cot, sent)
    forward(1, out_mer, in_mer, sent)
    backward(0, back_out, home_out, sent)
    backward(1, back_grad, home_grad, sent)


def local(fine, merge_gain, merge_w, attn_gain, qkv_w, proj_w, table, region, counts, cot):
    whole = pl.BlockSpec(memory_space=pltpu.VMEM)
    away = pl.BlockSpec(memory_space=pl.ANY)
    smem = pl.BlockSpec(memory_space=pltpu.SMEM)
    dma = pltpu.SemaphoreType.DMA

    def held(*shape, dtype=BF16):
        return pltpu.VMEM(shape, dtype)

    out, grad_fine = pl.pallas_call(
        kernel,
        out_shape=[
            jax.ShapeDtypeStruct((288, 1024), BF16),
            jax.ShapeDtypeStruct((1152, 512), BF16),
        ],
        in_specs=[whole, whole, away, whole, away, away, whole, whole, smem, whole],
        out_specs=[whole, whole],
        scratch_shapes=[
            held(2048, 1024),
            held(1024, 3072),
            held(1024, 1024),
            dma((3, N_IDS)),
            dma((3, N_IDS)),
            dma((3,)),
            dma((2, 5)),
            dma((2, 5)),
            dma((2, 5)),
            dma((2, 5)),
            held(OUT_ROWS, 1152),
            held(OUT_ROWS, 1024),
            held(IN_ROWS, 1152),
            held(IN_ROWS, 1024),
            held(IN_ROWS, 1024),
            held(IN_ROWS, 1024),
            held(OUT_ROWS, 1024),
            held(OUT_ROWS, 1024),
            held(288, 2048),
            held(288, 1024),
            held(288, 1024),
            held(288, 1024),
            held(288, 1024),
            held(288, 3072),
            held(288, 1024),
            held(288, 1024),
            held(288, 3072),
            held(288, 1024, dtype=F32),
            held(288, 2048, dtype=F32),
            held(12, 16, 384, dtype=F32),
            held(48, 640),
            held(16, 144, 144, dtype=F32),
            held(2, 144, 144, dtype=F32),
            held(16, 128, dtype=F32),
        ],
        compiler_params=pltpu.CompilerParams(
            collective_id=0, has_side_effects=True, vmem_limit_bytes=56 << 20
        ),
        cost_estimate=pl.CostEstimate(
            flops=10_000_000_000, bytes_accessed=20_000_000, transcendentals=700_000
        ),
    )(
        fine.reshape(1152, 512),
        merge_gain.reshape(1, 2048),
        merge_w,
        attn_gain.reshape(1, 1024),
        qkv_w,
        proj_w,
        table,
        region,
        counts,
        cot.reshape(288, 1024),
    )
    return out.reshape(12, 24, 1024), grad_fine.reshape(24, 48, 512)


def solution(mesh):
    grid = P("lat", "lon", None)
    rows = P("lat", None)
    return jax.shard_map(
        local,
        mesh=mesh,
        in_specs=(grid, P(), rows, P(), rows, rows, P(), P("lat", "lon"), P(), grid),
        out_specs=(grid, grid),
        check_vma=False,
    )
```

profile of v0, /device:TPU:6, one launch (start us, length us, event | category | flops | bytes accessed | tf_op | source)
XLA Modules:
  0.0 102.6 jit_solution(7137569395464765335)
XLA Ops:
  0.6 98.9 %shard_map.113 = (bf16[288,1024]{1,0:T(8,128)(2,1)}, bf16[1152,512]{1,0:T(8,128)(2,1)}) custom-call(bf16[1152,512]{1,0:T(8,128)(2,1)} %bitcast.8, f32[1,2048]{1,0:T(1,128)} %bitcast.10, bf16[128,1024]{1,0:T(8,128)(2,1)} %merge_shard.1, f32[1,1024]{1,0:T(1,128)} %bitcast.11, bf16[64,3072]{1,0:T(8,128)(2,1)} %qkv_shard.1, bf16[64,1024]{1,0:T(8,128)(2,1)} %proj_shard.1, ...), custom_call_target="tpu_custom_call" | custom-call | flops 10000000000 | bytes 20000000 | tf_op jit(solution)/shard_map/pallas_call | solution.py:681
  99.5 0.0 copy-start
  99.5 2.0 %copy.14 = bf16[12,24,1024]{2,1,0:T(8,128)(2,1)} copy(bf16[12,24,1024]{2,1,0:T(8,128)(2,1)} %bitcast.7) | data formatting | bytes 1179648
  101.5 0.0 copy-done
  101.5 1.0 copy.15
Async XLA Ops:
  99.5 2.0 %copy-start = (bf16[1152,512]{1,0:T(8,128)(2,1)S(1)}, bf16[1152,512]{1,0:T(8,128)(2,1)}, u32[]{:S(2)}) copy-start(bf16[1152,512]{1,0:T(8,128)(2,1)} %get-tuple-element.5) | copy-start | bytes 3538948
where the time goes:
time: 103 us
  Pallas kernels  98.9 us (96%)
  local copies, waits for them, and re-layouts  3.03 us (3%)
    pallas_call x1, Pallas kernels, local(): pl.pallas_call(kernel, out_shape=[jax.ShapeDtypeStruct((288, 1024), BF16)...  98.9 us
    unnamed x4, local copies, waits for them, and re-layouts  3.03 us

commit v1 on v0

v1 whole, which is shorter than its diff:
```python
import functools

import jax
import jax.numpy as jnp
from jax import lax
from jax.experimental import pallas as pl
from jax.experimental.pallas import tpu as pltpu
from jax.sharding import PartitionSpec as P

MESH = pl.DeviceIdType.MESH
BF16 = jnp.bfloat16
F32 = jnp.float32
NORM_EPS = 1e-05
MASKED = -1000000000.0
NT = (((1,), (1,)), ((), ()))
TN = (((0,), (0,)), ((), ()))

KEYS = [(1, 0), (0, 3), (0, 1), (0, 2), (1, 3), (1, 1), (1, 2)]
CROSS = [(1, 0), (0, 3), (0, 1), (0, 2, 0), (0, 2, 1), (1, 3), (1, 1), (1, 2)]
RID = {("c",) + k: i for i, k in enumerate(CROSS)}
RID.update({("r",) + k: 8 + i for i, k in enumerate(KEYS)})
RID.update({("k",) + k: 15 + i for i, k in enumerate(KEYS)})
RID.update({("q",) + k: 22 + i for i, k in enumerate(KEYS)})
RID[("own",)] = 29
N_IDS = 30
OWN = 7
PLAN = [
    (0, 7, "ym"), (0, 7, "yp"), (0, 7, "xh"), (1, 7, "xh"), (2, 7, "xh"), (1, 7, "ym"), (1, 7, "core"), (1, 7, "yp"),
    (0, 1, "yp"), (0, 0, "yp"), (0, 2, "ym"), (0, 1, "zm"), (0, 0, "ym"), (0, 0, "zp"), (0, 2, "xl"), (2, 7, "yp"),
    (1, 0, "zm"), (0, 2, "core"), (1, 1, "yp"), (1, 2, "ym"), (1, 2, "zp"), (1, 0, "ym"), (1, 1, "xl"),
    (0, 9, "core"), (2, 0, "core"), (0, 3, "xl"), (0, 0, "core"), (0, 3, "xh"), (0, 3, "core"), "tag", (2, 7, "ym"),
    (2, 0, "yp"), "bl0", (0, 5, "zp"), (0, 1, "core"), (0, 4, "zm"), "pat1", (2, 0, "xl"), (1, 2, "core"),
    (2, 1, "yp"), (0, 4, "core"), (1, 1, "core"), (0, 8, "core"), (1, 0, "yp"), "Hc", "bl1", (0, 6, "zp"), "bl2",
    (1, 3, "xh"), (1, 3, "zp"), (0, 6, "core"), (0, 7, "core"), "pat2", (1, 10, "core"), (0, 13, "core"),
    (0, 12, "core"), (0, 5, "core"), (2, 4, "xl"), (0, 11, "core"), (1, 5, "zm"), (0, 14, "core"), (0, 10, "core"),
    (2, 2, "ym"), "pat0", (2, 2, "xl"), (2, 2, "core"), (2, 4, "core"), (1, 6, "zp"), (2, 8, "core"), (1, 9, "core"),
    (1, 6, "core"), (2, 7, "core"), (1, 4, "zm"), (2, 3, "zp"), (1, 8, "core"), (2, 3, "xh"), "fin0", (1, 5, "core"),
    (2, 0, "ym"), (1, 3, "core"), "merge", "Hm", (1, 4, "core"), (1, 0, "core"), (2, 5, "zm"), (2, 12, "core"),
    (2, 1, "zp"), (1, 13, "core"), (2, 1, "core"), "wHc", (2, 3, "core"), "basm", (1, 14, "core"), (1, 12, "core"),
    (2, 6, "xl"), (1, 11, "core"), "wincot", (2, 11, "core"), (2, 5, "core"), (2, 6, "core"), (2, 9, "core"), "wHm",
    (2, 10, "core"), "winmer", "fin1", (2, 14, "core"), (2, 13, "core"), "qkv", "fin2", "up",
]

TC, TL, BR, BL, BLX = 0, 1, 2, 3, 4
SLOT = ((0, 80), (80, 48), (128, 48), (176, 48), (224, 48))
IN_ROWS, OUT_ROWS = 272, 224


class Gather:
    def __init__(self, shards, fulls, send_sem, recv_sem, local_sem):
        self.shards, self.fulls = shards, fulls
        self.send_sem, self.recv_sem, self.local_sem = send_sem, recv_sem, local_sem
        lat, lon = lax.axis_index("lat"), lax.axis_index("lon")
        a, y, k = lat // 8, (lat // 2) % 4, lat % 2
        z, xlo = lon // 2, lon % 2
        self.a, self.y, self.k = a, y, k
        self.c = (xlo + a + z) % 2

        def at(a_, y_, k_):
            return a_ * 8 + y_ * 2 + k_

        self.near = dict(
            yp=(at(a, (y + 1) % 4, k), lon),
            ym=(at(a, (y + 3) % 4, k), lon),
            xh=(at(1 - a, y, k), z * 2 + (1 - xlo)),
            xl=(lat, z * 2 + (1 - xlo)),
            zp=(lat, ((z + 1) % 8) * 2 + xlo),
            zm=(lat, ((z + 7) % 8) * 2 + xlo),
            core=(at(a, y, 1 - k), lon),
        )
        self.sent, self.local, self.here = [], {}, set()
        self.count = [0] * len(shards)

    def rows(self, w, key, half, core):
        r = self.shards[w].shape[0]
        a = self.a if key[0] == 0 else 1 - self.a
        s = a * 8 + ((self.y + key[1]) % 4) * 2 + core
        if half is None:
            return pl.ds(pl.multiple_of(s * r, r), r)
        off, n = half * (r // 2), r // 2
        if len(key) == 3:
            off, n = off + key[2] * (r // 4), r // 4
        return pl.ds(pl.multiple_of(s * r + off, n), n)

    def copy(self, w, rid, src, dst, dev, i):
        return pltpu.make_async_remote_copy(
            src_ref=src,
            dst_ref=dst,
            send_sem=self.send_sem.at[w, i],
            recv_sem=self.recv_sem.at[w, RID[rid]],
            device_id=dev,
            device_id_type=MESH,
        )

    def send(self, w, where, to, rid, src=None):
        full = self.fulls[w]
        i = self.count[w]
        self.count[w] += 1
        src = full.at[where] if src is None else src
        cp = self.copy(w, rid, src, full.at[where], self.near[to], i)
        cp.start()
        self.sent.append(cp)

    def recv(self, w, rid, where):
        part = self.fulls[w].at[where]
        self.copy(w, rid, part, part, self.near["core"], 0).wait_recv()

    def source(self, w, src):
        if src == OWN:
            return self.rows(w, (0, 0), None, self.k)
        key = KEYS[src % 8]
        half = self.c if src < 8 else 1 - self.c
        where = self.rows(w, key, half, self.k)
        if (w, src) not in self.here:
            self.here.add((w, src))
            if src >= 8:
                self.recv(w, ("r",) + key, where)
            elif key == (0, 2):
                for part in (0, 1):
                    self.recv(w, ("c", 0, 2, part), self.rows(w, (0, 2, part), half, self.k))
            else:
                self.recv(w, ("c",) + key, where)
        return where

    def hop(self, w, src, to):
        c, k = self.c, self.k
        where = self.source(w, src)
        if src == OWN:
            shard = self.shards[w]
            r = shard.shape[0] // 2
            if to == "core":
                self.send(w, where, to, ("own",), shard)
                cp = pltpu.make_async_copy(shard, self.fulls[w].at[where], self.local_sem.at[w])
                cp.start()
                self.local[w] = cp
            else:
                half = shard.at[pl.ds(pl.multiple_of(c * r, r), r)]
                rid = {"xh": (1, 0), "yp": (0, 3), "ym": (0, 1)}[to]
                self.send(w, self.rows(w, (0, 0), c, k), to, ("c",) + rid, half)
            return
        key = KEYS[src % 8]
        if to == "core":
            self.send(w, where, to, (("k",) if src < 8 else ("q",)) + key)
        elif to in ("zp", "zm", "xl"):
            self.send(w, where, to, ("r",) + key)
        elif key == (1, 0):
            self.send(w, where, to, ("c", 1, 3 if to == "yp" else 1))
        elif key == (0, 2):
            self.send(w, where, to, ("c", 1, 2))
        else:
            part = 0 if to == "yp" else 1
            self.send(w, self.rows(w, key + (part,), c, k), to, ("c", 0, 2, part))

    def fin(self, w):
        self.recv(w, ("own",), self.rows(w, (0, 0), None, 1 - self.k))
        for key in KEYS:
            self.recv(w, ("k",) + key, self.rows(w, key, self.c, 1 - self.k))
            self.recv(w, ("q",) + key, self.rows(w, key, 1 - self.c, 1 - self.k))
        self.local[w].wait()

    def drain(self):
        for cp in self.sent:
            cp.wait_send()


def over12(v):
    return (v * 171) >> 11


def over6(v):
    return (v * 171) >> 10


def window_source(d, lat):
    second = d >= 144
    e = jnp.where(second, d - 144, d)
    r = over12(e)
    c = e - 12 * r
    none = jnp.full(d.shape, -1, jnp.int32)
    lats = jnp.zeros(d.shape, jnp.int32) + lat
    upper = r < 6
    left = c < 6
    edge = (r - 6) * 6 + (c - 6)
    last = lats == 15
    first = lats == 0
    own_a = jnp.where(upper, (6 + r) * 24 + 6 + c, jnp.where(last & left, r * 24 + 18 + c, none))
    in_a = jnp.where(
        upper,
        none,
        jnp.where(last, jnp.where(left, none, SLOT[BLX][0] + edge), (r - 6) * 12 + c),
    )
    own_b = jnp.where(
        upper,
        jnp.where(first, r * 24 + 6 + c, none),
        jnp.where(left, (r - 6) * 24 + 18 + c, none),
    )
    in_top = jnp.where(left, SLOT[BR][0] + r * 6 + c, SLOT[BL][0] + r * 6 + c - 6)
    in_b = jnp.where(
        upper,
        jnp.where(first, none, in_top),
        jnp.where(left, none, SLOT[TL][0] + edge),
    )
    return jnp.where(second, own_b, own_a), jnp.where(second, in_b, in_a)


def slot_source(s):
    none = jnp.full(s.shape, -1, jnp.int32)
    r12 = over12(s)
    tc = jnp.where(s < 72, r12 * 24 + 6 + s - 12 * r12, none)

    def corner(base, row, col):
        t = s - base
        r = over6(t)
        return jnp.where(t < 36, (row + r) * 24 + col + t - 6 * r, none)

    tl, br, bl = corner(80, 0, 0), corner(128, 6, 18), corner(176, 6, 0)
    return jnp.where(s < 80, tc, jnp.where(s < 128, tl, jnp.where(s < 176, br, bl)))


def column(n):
    return lax.broadcasted_iota(jnp.int32, (n, 1), 0)


def line(n):
    return lax.broadcasted_iota(jnp.int32, (1, n), 1)


def pick(source, rows, cols):
    axis = 1 if source.shape[1] == 1 else 0
    place = lax.broadcasted_iota(jnp.int32, (rows, cols), axis)
    return (source == place).astype(F32).astype(BF16)


def dot(a, b):
    return jnp.dot(a, b, preferred_element_type=F32)


def dot_nt(a, b):
    return lax.dot_general(a, b, NT, preferred_element_type=F32)


def dot_tn(a, b):
    return lax.dot_general(a, b, TN, preferred_element_type=F32)


def norm_rows(v):
    n = v.shape[-1]
    centred = v - jnp.sum(v, axis=-1, keepdims=True) * (1.0 / n)
    inv = lax.rsqrt(jnp.sum(centred * centred, axis=-1, keepdims=True) * (1.0 / n) + NORM_EPS)
    return centred * inv, inv


def kernel(
    fine_hbm,
    merge_gain_hbm,
    merge_shard,
    attn_gain_hbm,
    qkv_shard,
    proj_shard,
    table_hbm,
    region_hbm,
    counts_hbm,
    cot_hbm,
    out,
    grad_fine,
    merge,
    qkv_w,
    proj,
    g_send,
    g_recv,
    g_local,
    f_send,
    f_recv,
    b_send,
    b_recv,
    out_cot,
    out_mer,
    in_cot,
    in_mer,
    back_out,
    back_grad,
    home_out,
    home_grad,
    patch_n,
    patch_f,
    patch_inv,
    merged_home,
    win_mer,
    win_cot,
    normed,
    proj_all,
    upstream,
    attended,
    grad_all,
    wide,
    grad_patch,
    lines,
    split,
    bias,
    mask,
    tag_pad,
    live,
    fine,
    cot,
    merge_gain,
    attn_gain,
    table,
    region,
    counts,
    load_sem,
    score_buf,
    grads_buf,
    low_buf,
    logit_buf,
):
    lat, lon = lax.axis_index("lat"), lax.axis_index("lon")
    up = ((lat + 15) % 16, lon)
    down = ((lat + 1) % 16, lon)
    left = (lat, (lon + 15) % 16)
    right = (lat, (lon + 1) % 16)
    down_left = ((lat + 1) % 16, (lon + 15) % 16)
    up_right = ((lat + 15) % 16, (lon + 1) % 16)
    gather = Gather((merge_shard, qkv_shard, proj_shard), (merge, qkv_w, proj), g_send, g_recv, g_local)

    pairs = dict(
        region=(region_hbm, region),
        counts=(counts_hbm, counts),
        cot=(cot_hbm, cot),
        fine=(fine_hbm, fine),
        merge_gain=(merge_gain_hbm, merge_gain),
        table=(table_hbm, table),
        attn_gain=(attn_gain_hbm, attn_gain),
    )
    loads = {
        name: pltpu.make_async_copy(src, dst, load_sem.at[i])
        for i, (name, (src, dst)) in enumerate(pairs.items())
    }
    for cp in loads.values():
        cp.start()

    def loaded(*names):
        for name in names:
            if name in loads:
                loads.pop(name).wait()

    for ref in (in_cot, in_mer, home_out, home_grad):
        ref[...] = jnp.zeros_like(ref)
    barrier = pltpu.get_barrier_semaphore()
    partners = list(gather.near.values()) + [up, down, left, right, down_left, up_right]
    for dev in partners:
        pl.semaphore_signal(barrier, inc=1, device_id=dev, device_id_type=MESH)
    pl.semaphore_wait(barrier, len(partners))

    not_first, not_last, is_last = lat > 0, lat < 15, lat == 15

    def forward(m, src, dst, do):
        def go(slot_from, slot_to, dev):
            f0, n = SLOT[slot_from]
            t0 = SLOT[slot_to][0]
            do(
                pltpu.make_async_remote_copy(
                    src_ref=src.at[pl.ds(f0, n)],
                    dst_ref=dst.at[pl.ds(t0, n)],
                    send_sem=f_send.at[m, slot_from],
                    recv_sem=f_recv.at[m, slot_to],
                    device_id=dev,
                    device_id_type=MESH,
                )
            )

        go(TL, TL, left)

        @pl.when(not_first)
        def _():
            go(TC, TC, up)

        @pl.when(not_last)
        def _():
            go(BR, BR, down)
            go(BL, BL, down_left)

        @pl.when(is_last)
        def _():
            go(BL, BLX, left)

    def forward_recv(m, dst):
        def got(slot):
            f0, n = SLOT[slot]
            part = dst.at[pl.ds(f0, n)]
            pltpu.make_async_remote_copy(
                src_ref=part,
                dst_ref=part,
                send_sem=f_send.at[m, 0],
                recv_sem=f_recv.at[m, slot],
                device_id=right,
                device_id_type=MESH,
            ).wait_recv()

        got(TL)

        @pl.when(not_last)
        def _():
            got(TC)

        @pl.when(not_first)
        def _():
            got(BR)
            got(BL)

        @pl.when(is_last)
        def _():
            got(BLX)

    def backward(m, w, src, dst, do):
        def go(slot_from, slot_to, dev):
            f0, n = SLOT[slot_from]
            t0 = SLOT[slot_to][0]
            do(
                pltpu.make_async_remote_copy(
                    src_ref=src.at[pl.ds(f0, n)],
                    dst_ref=dst.at[pl.ds(t0, n)],
                    send_sem=b_send.at[m, slot_from],
                    recv_sem=b_recv.at[m, slot_to],
                    device_id=dev,
                    device_id_type=MESH,
                )
            )

        if w == 1:
            go(TL, TL, right)

            @pl.when(not_first)
            def _():
                go(BL, BL, up_right)
                go(BR, BR, up)

        else:

            @pl.when(not_last)
            def _():
                go(TC, TC, down)

            @pl.when(is_last)
            def _():
                go(BLX, BL, right)

    def backward_recv(m, dst):
        def got(slot):
            f0, n = SLOT[slot]
            part = dst.at[pl.ds(f0, n)]
            pltpu.make_async_remote_copy(
                src_ref=part,
                dst_ref=part,
                send_sem=b_send.at[m, 0],
                recv_sem=b_recv.at[m, slot],
                device_id=right,
                device_id_type=MESH,
            ).wait_recv()

        got(TL)
        got(BL)

        @pl.when(not_first)
        def _():
            got(TC)

        @pl.when(not_last)
        def _():
            got(BR)

    def start(cp):
        cp.start()

    def sent(cp):
        cp.wait_send()

    cell = column(288)
    cell_row = (cell * 171) >> 12
    v = {}

    def step_tag():
        loaded("region", "counts", "cot")
        tag_pad[...] = jnp.zeros_like(tag_pad)
        tag_pad[0:12, 0:24] = (region[...] + 1).astype(F32)
        cell_col = cell - 24 * cell_row
        row_pick = (cell_row == lax.broadcasted_iota(jnp.int32, (288, 16), 1)).astype(F32).astype(BF16)
        tags = dot(row_pick, tag_pad[...].astype(BF16))
        lanes128 = lax.broadcasted_iota(jnp.int32, (288, 128), 1)
        tag = jnp.sum(jnp.where(lanes128 == cell_col, tags, 0.0), axis=-1, keepdims=True)
        held_rows = jnp.sum(jnp.where(line(16) == lat, counts[...], 0), axis=-1, keepdims=True)
        tag = tag * (cell_row < held_rows).astype(F32)
        v["tag_home"] = jnp.broadcast_to(tag, (288, 128)).astype(BF16)
        v["to_slots"] = pick(slot_source(column(OUT_ROWS)), OUT_ROWS, 288)
        out_cot[:, 0:1024] = dot(v["to_slots"], cot[...]).astype(BF16)
        out_cot[:, 1024:1152] = dot(v["to_slots"], v["tag_home"]).astype(BF16)

    def step_send_cot():
        forward(0, out_cot, in_cot, start)

    o = column(192)
    block = jnp.where(o < 48, 0, jnp.where(o < 96, 1, jnp.where(o < 144, 2, 3)))
    within = o - 48 * block
    wr = (within >= 24).astype(jnp.int32)
    wc = within - 24 * wr
    to_blocks = pick((2 * wr + (block & 1)) * 48 + 2 * wc + (block >> 1), 192, 192)

    def patches(g, _):
        raw = dot(to_blocks, fine[pl.ds(pl.multiple_of(g * 192, 192), 192), :])
        parts = [raw[48 * b : 48 * b + 48] for b in range(4)]
        average = sum(jnp.sum(p, axis=-1, keepdims=True) for p in parts) * (1.0 / 2048)
        parts = [p - average for p in parts]
        spread = sum(jnp.sum(p * p, axis=-1, keepdims=True) for p in parts) * (1.0 / 2048)
        inv = lax.rsqrt(spread + NORM_EPS)
        at = pl.ds(pl.multiple_of(g * 48, 48), 48)
        for b in range(4):
            gain = merge_gain[:, 512 * b : 512 * b + 512]
            normal = parts[b] * inv
            patch_f[at, 512 * b : 512 * b + 512] = normal
            patch_n[at, 512 * b : 512 * b + 512] = (normal * gain).astype(BF16)
        patch_inv[at, :] = jnp.broadcast_to(inv, (48, 128))
        return 0

    def step_patches(part):
        loaded("fine", "merge_gain")
        lax.fori_loop(2 * part, 2 * part + 2, patches, 0)

    def bias_lines(c, _):
        lane = line(384)
        u = over12(lane)
        index = jnp.where(lane < 276, u * 23 + (lane - 12 * u) - c + 11, -1)
        three = dot(split[...], pick(index, 640, 384))
        lines[c] = three[0:16] + three[16:32] + three[32:48]
        return 0

    def step_lines(part):
        if "table" in loads:
            loaded("table")
            t = table[...]
            high = t.astype(BF16)
            rest = t - high.astype(F32)
            middle = rest.astype(BF16)
            split[...] = jnp.zeros_like(split)
            split[0:16, 0:529] = high
            split[16:32, 0:529] = middle
            split[32:48, 0:529] = (rest - middle.astype(F32)).astype(BF16)
        lax.fori_loop(4 * part, 4 * part + 4, bias_lines, 0)

    def step_bias():
        for h in range(16):
            some = lines[:, h, :]
            for r in range(12):
                at = 144 * h + 12 * r
                bias[at : at + 12, :] = some[:, 12 * (11 - r) : 12 * (11 - r) + 144]

    def step_merge():
        def merge_tile(n, _):
            at = pl.ds(pl.multiple_of(n * 512, 512), 512)
            merged_home[:, at] = dot(patch_n[...], merge[:, at]).astype(BF16)
            return 0

        lax.fori_loop(0, 2, merge_tile, 0)
        out_mer[...] = dot(v["to_slots"], merged_home[...]).astype(BF16)

    def step_send_merged():
        forward(1, out_mer, in_mer, start)

    def owner():
        own, came = window_source(column(288), lat)
        return pick(own, 288, 288), pick(came, 288, IN_ROWS)

    def step_window_cot():
        from_home, from_slots = owner()
        win_cot[...] = (dot(from_home, cot[...]) + dot(from_slots, in_cot[:, 0:1024])).astype(BF16)
        win_tag = dot(from_home, v["tag_home"]) + dot(from_slots, in_cot[:, 1024:1152])
        d = lax.broadcasted_iota(jnp.int32, (288, 128), 0)
        apart = ((lat == 15) & (d >= 72) & (d < 144)) | ((lat == 0) & (d >= 144) & (d < 216))
        alive = (win_tag > 0).astype(F32)
        live[...] = alive
        win_tag = win_tag + 8.0 * alive * apart.astype(F32)
        for w in range(2):
            at = slice(144 * w, 144 * w + 144)
            key_tag = win_tag[at, 0:1]
            query_tag = jnp.transpose(win_tag[at])[0:1]
            allowed = (key_tag == query_tag) & (key_tag > 0)
            mask[w] = jnp.where(allowed, 0.0, MASKED)

    def step_window_merged():
        from_home, from_slots = owner()
        win_mer[...] = (dot(from_home, merged_home[...]) + dot(from_slots, in_mer[...])).astype(BF16)

        loaded("attn_gain")

        def norm_chunk(g, _):
            at = pl.ds(pl.multiple_of(g * 144, 144), 144)
            normed[at, :] = (norm_rows(win_mer[at, :].astype(F32))[0] * attn_gain[...]).astype(BF16)
            return 0

        lax.fori_loop(0, 2, norm_chunk, 0)

    def step_qkv():
        def qkv_tile(n, _):
            at = pl.ds(pl.multiple_of(n * 1024, 1024), 1024)
            proj_all[:, at] = dot(normed[...], qkv_w[:, at]).astype(BF16)
            return 0

        lax.fori_loop(0, 3, qkv_tile, 0)

    def step_upstream():
        upstream[...] = (dot_nt(win_cot[...], proj[...]) * live[:, 0:1]).astype(BF16)

    steps = dict(
        tag=step_tag,
        Hc=step_send_cot,
        pat0=lambda: step_patches(0),
        pat1=lambda: step_patches(1),
        pat2=lambda: step_patches(2),
        bl0=lambda: step_lines(0),
        bl1=lambda: step_lines(1),
        bl2=lambda: step_lines(2),
        basm=step_bias,
        fin0=lambda: gather.fin(0),
        fin1=lambda: gather.fin(1),
        fin2=lambda: gather.fin(2),
        merge=step_merge,
        Hm=step_send_merged,
        wHc=lambda: forward_recv(0, in_cot),
        wHm=lambda: forward_recv(1, in_mer),
        wincot=step_window_cot,
        winmer=step_window_merged,
        qkv=step_qkv,
        up=step_upstream,
    )
    for op in PLAN:
        if isinstance(op, str):
            steps[op]()
        else:
            gather.hop(*op)

    low_half = lax.broadcasted_iota(jnp.int32, (144, 128), 1) < 64
    none = jnp.zeros((144, 128), BF16)

    def window_rows(w):
        return pl.ds(144 * w, 144)

    def features(w, pair):
        off = pl.multiple_of(pair * 128, 128)
        rows = window_rows(w)
        q = proj_all[rows, pl.ds(off, 128)] * jnp.asarray(0.125, BF16)
        k = proj_all[rows, pl.ds(1024 + off, 128)]
        v_ = proj_all[rows, pl.ds(2048 + off, 128)]
        return q, k, v_, upstream[rows, pl.ds(off, 128)]

    def stage_products(w, pair, slot):
        q, k, v_, u = features(w, pair)
        two_k = jnp.concatenate([jnp.where(low_half, k, none), jnp.where(low_half, none, k)])
        two_v = jnp.concatenate([jnp.where(low_half, v_, none), jnp.where(low_half, none, v_)])
        score_buf[slot] = dot_nt(two_k, q)
        grads_buf[slot] = dot_nt(two_v, u)

    def stage_softmax(w, pair, slot):
        offsets = bias[pl.ds(pl.multiple_of(pair * 288, 288), 288), :]
        scores = (score_buf[slot] + offsets).reshape(2, 144, 144) + mask[w][None]
        powers = jnp.exp(scores - jnp.max(scores, axis=1, keepdims=True))
        probs = powers * (1.0 / jnp.sum(powers, axis=1, keepdims=True))
        grads = grads_buf[slot].reshape(2, 144, 144)
        logits = probs * (grads - jnp.sum(probs * grads, axis=1, keepdims=True))
        low_buf[slot] = probs.astype(BF16).reshape(288, 144)
        logit_buf[slot] = logits.astype(BF16).reshape(288, 144)

    def stage_sums(w, pair, slot):
        off = pl.multiple_of(pair * 128, 128)
        rows = window_rows(w)
        q, k, v_, u = features(w, pair)
        low, logits = low_buf[slot], logit_buf[slot]

        def both(m, x):
            y = dot(m, x)
            return jnp.where(low_half, y[0:144], y[144:288])

        def turned(m):
            return jnp.concatenate([m[0:144].T, m[144:288].T])

        alive = live[144 * w : 144 * w + 144, :]
        attended[rows, pl.ds(off, 128)] = (both(turned(low), v_) * alive).astype(BF16)
        grad_all[rows, pl.ds(off, 128)] = (both(turned(logits), k) * 0.125).astype(BF16)
        grad_all[rows, pl.ds(1024 + off, 128)] = both(logits, q).astype(BF16)
        grad_all[rows, pl.ds(2048 + off, 128)] = both(low, u).astype(BF16)

    def pairs_of(w):
        def two(i, _):
            for b in range(2):
                j = 2 * i + b
                stage_sums(w, j, b)
                stage_softmax(w, j + 1, 1 - b)
                stage_products(w, j + 2, b)
            return 0

        lax.fori_loop(0, 3, two, 0)

    def slots_of(w):
        _, came = window_source(line(144) + 144 * w, lat)
        if w == 1:
            return pick(jnp.where(came >= 0, came - SLOT[TL][0], came), 144, 144)
        came = jnp.where(came >= SLOT[BLX][0], came - SLOT[BLX][0] + 80, came)
        return pick(came, 128, 144)

    def put_slots(w, dst, cells):
        moved = dot(slots_of(w), cells).astype(BF16)
        if w == 1:
            dst[80:224] = moved
        else:
            dst[0:80] = moved[0:80]
            dst[224:272] = moved[80:128]

    def window_tail(w):
        rows = window_rows(w)
        total = win_mer[rows, :].astype(F32) + dot(attended[rows, :], proj[...])
        normed[rows, :] = total.astype(BF16)
        put_slots(w, back_out, normed[rows, :])
        backward(0, w, back_out, home_out, start)
        for n in range(2):
            wide[rows, 512 * n : 512 * n + 512] = dot_nt(grad_all[rows, :], qkv_w[512 * n : 512 * n + 512, :])
        normal, inv = norm_rows(win_mer[rows, :].astype(F32))
        weighted = wide[rows, :] * attn_gain[...]
        first = jnp.sum(weighted, axis=-1, keepdims=True) * (1.0 / 1024)
        second = jnp.sum(weighted * normal, axis=-1, keepdims=True) * (1.0 / 1024)
        back = win_cot[rows, :].astype(F32) + inv * (weighted - first - normal * second)
        win_cot[rows, :] = back.astype(BF16)
        put_slots(w, back_grad, win_cot[rows, :])
        backward(1, w, back_grad, home_grad, start)

    stage_products(1, 0, 0)
    stage_products(1, 1, 1)
    stage_softmax(1, 0, 0)
    pairs_of(1)
    stage_sums(1, 6, 0)
    stage_softmax(1, 7, 1)
    stage_products(0, 0, 0)
    stage_sums(1, 7, 1)
    stage_softmax(0, 0, 0)
    stage_products(0, 1, 1)
    window_tail(1)
    pairs_of(0)
    stage_sums(0, 6, 0)
    stage_softmax(0, 7, 1)
    stage_sums(0, 7, 1)
    window_tail(0)

    own_l, _ = window_source(line(288), lat)
    to_home = pick(own_l, 288, 288)
    slots_home = pick(slot_source(line(OUT_ROWS)), 288, OUT_ROWS)
    backward_recv(0, home_out)
    out[...] = (dot(to_home, normed[...]) + dot(slots_home, home_out[...])).astype(BF16)
    backward_recv(1, home_grad)
    merged_home[...] = (dot(to_home, win_cot[...]) + dot(slots_home, home_grad[...])).astype(BF16)

    def patch_tile(n, _):
        at = pl.ds(pl.multiple_of(n * 1024, 1024), 1024)
        grad_patch[:, at] = dot_nt(merged_home[...], merge[at, :])
        return 0

    lax.fori_loop(0, 2, patch_tile, 0)

    def patch_back(g, _):
        at = pl.ds(pl.multiple_of(g * 48, 48), 48)
        parts = [patch_f[at, 512 * b : 512 * b + 512] for b in range(4)]
        inv = patch_inv[at, 0:1]
        weighted = [
            grad_patch[at, 512 * b : 512 * b + 512] * merge_gain[:, 512 * b : 512 * b + 512]
            for b in range(4)
        ]
        first = sum(jnp.sum(x, axis=-1, keepdims=True) for x in weighted) * (1.0 / 2048)
        second = sum(
            jnp.sum(x * n, axis=-1, keepdims=True) for x, n in zip(weighted, parts)
        ) * (1.0 / 2048)
        back = [(inv * (x - first - n * second)).astype(BF16) for x, n in zip(weighted, parts)]
        tokens = dot_tn(to_blocks, jnp.concatenate(back, axis=0))
        grad_fine[pl.ds(pl.multiple_of(g * 192, 192), 192), :] = tokens.astype(BF16)
        return 0

    lax.fori_loop(0, 6, patch_back, 0)

    gather.drain()
    forward(0, out_cot, in_cot, sent)
    forward(1, out_mer, in_mer, sent)
    for w in range(2):
        backward(0, w, back_out, home_out, sent)
        backward(1, w, back_grad, home_grad, sent)


def local(fine, merge_gain, merge_w, attn_gain, qkv_w, proj_w, table, region, counts, cot):
    whole = pl.BlockSpec(memory_space=pltpu.VMEM)
    away = pl.BlockSpec(memory_space=pl.ANY)
    dma = pltpu.SemaphoreType.DMA

    def held(*shape, dtype=BF16):
        return pltpu.VMEM(shape, dtype)

    out, grad_fine = pl.pallas_call(
        kernel,
        out_shape=[
            pltpu.VMEM((288, 1024), BF16),
            pltpu.VMEM((1152, 512), BF16),
        ],
        in_specs=[away] * 10,
        out_specs=[whole, whole],
        scratch_shapes=[
            held(2048, 1024),
            held(1024, 3072),
            held(1024, 1024),
            dma((3, N_IDS)),
            dma((3, N_IDS)),
            dma((3,)),
            dma((2, 5)),
            dma((2, 5)),
            dma((2, 5)),
            dma((2, 5)),
            held(OUT_ROWS, 1152),
            held(OUT_ROWS, 1024),
            held(IN_ROWS, 1152),
            held(IN_ROWS, 1024),
            held(IN_ROWS, 1024),
            held(IN_ROWS, 1024),
            held(OUT_ROWS, 1024),
            held(OUT_ROWS, 1024),
            held(288, 2048),
            held(288, 2048, dtype=F32),
            held(288, 128, dtype=F32),
            held(288, 1024),
            held(288, 1024),
            held(288, 1024),
            held(288, 1024),
            held(288, 3072),
            held(288, 1024),
            held(288, 1024),
            held(288, 3072),
            held(288, 1024, dtype=F32),
            held(288, 2048, dtype=F32),
            held(12, 16, 384, dtype=F32),
            held(48, 640),
            held(2304, 144, dtype=F32),
            held(2, 144, 144, dtype=F32),
            held(16, 128, dtype=F32),
            held(288, 128, dtype=F32),
            held(1152, 512),
            held(288, 1024),
            held(1, 2048, dtype=F32),
            held(1, 1024, dtype=F32),
            held(16, 529, dtype=F32),
            held(12, 24, dtype=jnp.int32),
            held(1, 16, dtype=jnp.int32),
            dma((7,)),
            held(2, 288, 144, dtype=F32),
            held(2, 288, 144, dtype=F32),
            held(2, 288, 144),
            held(2, 288, 144),
        ],
        compiler_params=pltpu.CompilerParams(
            collective_id=0, has_side_effects=True, vmem_limit_bytes=60 << 20
        ),
        cost_estimate=pl.CostEstimate(
            flops=10_000_000_000, bytes_accessed=20_000_000, transcendentals=700_000
        ),
    )(
        fine.reshape(1152, 512),
        merge_gain.reshape(1, 2048),
        merge_w,
        attn_gain.reshape(1, 1024),
        qkv_w,
        proj_w,
        table,
        region,
        counts.reshape(1, 16),
        cot.reshape(288, 1024),
    )
    return out.reshape(12, 24, 1024), grad_fine.reshape(24, 48, 512)


def solution(mesh):
    grid = P("lat", "lon", None)
    rows = P("lat", None)
    return jax.shard_map(
        local,
        mesh=mesh,
        in_specs=(grid, P(), rows, P(), rows, rows, P(), P("lat", "lon"), P(), grid),
        out_specs=(grid, grid),
        check_vma=False,
    )
```

time: 103 us -> 80 us (0.78)
  Pallas kernels: 98.9 us -> 77.5 us
  local copies, waits for them, and re-layouts: 3.03 us -> 1.83 us
    pallas_call x1, Pallas kernels: 98.9 us -> 77.5 us  [local(): pl.pallas_call(kernel, out_shape=[pltpu.VMEM((288, 1024), BF16), pltpu.VM...]
    unnamed x4 -> x2, local copies, waits for them, and re-layouts: 3.03 us -> 1.83 us
where the time goes in v1:
time: 80 us; the launch traced here: 79.9 us
  Pallas kernels  77.5 us (97%)
  local copies, waits for them, and re-layouts  1.83 us (2%)
    pallas_call x1, Pallas kernels, local(): pl.pallas_call(kernel, out_shape=[pltpu.VMEM((288, 1024), BF16), pltpu.VM...  77.5 us
    unnamed x2, local copies, waits for them, and re-layouts  1.83 us

profile of v1, /device:TPU:6, one launch (start us, length us, event | category | flops | bytes accessed | tf_op | source)
XLA Modules:
  0.0 79.9 jit_solution(9286039656352145587)
XLA Ops:
  0.6 77.5 %shard_map.113 = (bf16[288,1024]{1,0:T(8,128)(2,1)S(1)}, bf16[1152,512]{1,0:T(8,128)(2,1)S(1)}) custom-call(bf16[1152,512]{1,0:T(8,128)(2,1)} %bitcast.9, f32[1,2048]{1,0:T(1,128)} %bitcast.11, bf16[128,1024]{1,0:T(8,128)(2,1)} %merge_shard.1, f32[1,1024]{1,0:T(1,128)} %bitcast.12, bf16[64,3072]{1,0:T(8,128)(2,1)} %qkv_shard.1, bf16[64,1024]{1,0:T(8,128)(2,1)} %proj_shard.1, ...), custom_call_target="tpu_custom_call" | custom-call | flops 10000000000 | bytes 20000000 | tf_op jit(solution)/shard_map/pallas_call | solution.py:799
  78.1 0.8 %copy.14 = bf16[12,24,1024]{2,1,0:T(8,128)(2,1)} copy(bf16[12,24,1024]{2,1,0:T(8,128)(2,1)S(1)} %bitcast.8) | data formatting | bytes 1179648
  78.9 1.0 %copy.15 = bf16[24,48,512]{2,1,0:T(8,128)(2,1)} copy(bf16[24,48,512]{2,1,0:T(8,128)(2,1)S(1)} %bitcast.7) | data formatting | bytes 2359296

commit v2 on v1

--- a/solution.py
+++ b/solution.py
@@ -25,20 +25,21 @@
 N_IDS = 30
 OWN = 7
 PLAN = [
-    (0, 7, "ym"), (0, 7, "yp"), (0, 7, "xh"), (1, 7, "xh"), (2, 7, "xh"), (1, 7, "ym"), (1, 7, "core"), (1, 7, "yp"),
-    (0, 1, "yp"), (0, 0, "yp"), (0, 2, "ym"), (0, 1, "zm"), (0, 0, "ym"), (0, 0, "zp"), (0, 2, "xl"), (2, 7, "yp"),
-    (1, 0, "zm"), (0, 2, "core"), (1, 1, "yp"), (1, 2, "ym"), (1, 2, "zp"), (1, 0, "ym"), (1, 1, "xl"),
-    (0, 9, "core"), (2, 0, "core"), (0, 3, "xl"), (0, 0, "core"), (0, 3, "xh"), (0, 3, "core"), "tag", (2, 7, "ym"),
-    (2, 0, "yp"), "bl0", (0, 5, "zp"), (0, 1, "core"), (0, 4, "zm"), "pat1", (2, 0, "xl"), (1, 2, "core"),
-    (2, 1, "yp"), (0, 4, "core"), (1, 1, "core"), (0, 8, "core"), (1, 0, "yp"), "Hc", "bl1", (0, 6, "zp"), "bl2",
-    (1, 3, "xh"), (1, 3, "zp"), (0, 6, "core"), (0, 7, "core"), "pat2", (1, 10, "core"), (0, 13, "core"),
-    (0, 12, "core"), (0, 5, "core"), (2, 4, "xl"), (0, 11, "core"), (1, 5, "zm"), (0, 14, "core"), (0, 10, "core"),
-    (2, 2, "ym"), "pat0", (2, 2, "xl"), (2, 2, "core"), (2, 4, "core"), (1, 6, "zp"), (2, 8, "core"), (1, 9, "core"),
-    (1, 6, "core"), (2, 7, "core"), (1, 4, "zm"), (2, 3, "zp"), (1, 8, "core"), (2, 3, "xh"), "fin0", (1, 5, "core"),
-    (2, 0, "ym"), (1, 3, "core"), "merge", "Hm", (1, 4, "core"), (1, 0, "core"), (2, 5, "zm"), (2, 12, "core"),
-    (2, 1, "zp"), (1, 13, "core"), (2, 1, "core"), "wHc", (2, 3, "core"), "basm", (1, 14, "core"), (1, 12, "core"),
-    (2, 6, "xl"), (1, 11, "core"), "wincot", (2, 11, "core"), (2, 5, "core"), (2, 6, "core"), (2, 9, "core"), "wHm",
-    (2, 10, "core"), "winmer", "fin1", (2, 14, "core"), (2, 13, "core"), "qkv", "fin2", "up",
+    (0, 7, "ym"), (2, 7, "xh"), (2, 7, "core"), (0, 7, "yp"), (1, 7, "yp"), (0, 7, "xh"), (1, 7, "xh"), (1, 7, "ym"),
+    (0, 2, "zm"), "bl2", (0, 2, "ym"), (0, 1, "xl"), (0, 1, "yp"), (0, 0, "ym"), (0, 0, "yp"), (2, 7, "yp"),
+    (0, 0, "zp"), "tag", (1, 2, "zp"), (2, 7, "ym"), (1, 1, "core"), (1, 1, "xl"), (0, 3, "xh"), (0, 1, "core"),
+    (0, 3, "zm"), (2, 0, "core"), (0, 9, "core"), "pat0", (1, 2, "core"), (1, 7, "core"), (1, 1, "yp"), (1, 2, "ym"),
+    (1, 0, "yp"), (2, 0, "yp"), (0, 5, "zp"), (0, 4, "zm"), (0, 0, "core"), (2, 0, "xl"), (0, 2, "core"), "pat2",
+    (2, 2, "ym"), (1, 0, "zp"), (0, 6, "xl"), (2, 2, "core"), (1, 0, "ym"), (0, 11, "core"), (1, 3, "zm"),
+    (0, 7, "core"), (0, 8, "core"), (2, 1, "core"), (0, 4, "core"), (0, 3, "core"), (2, 1, "yp"), (0, 6, "core"),
+    (1, 3, "xh"), "Hc", (1, 9, "core"), (0, 10, "core"), (0, 12, "core"), (0, 5, "core"), (0, 13, "core"), "pat1",
+    (2, 0, "ym"), (0, 14, "core"), (2, 1, "zp"), (1, 4, "zp"), "fin0", (1, 5, "zm"), (1, 4, "core"), "merge",
+    (1, 6, "core"), (2, 3, "xh"), "Hm", (1, 0, "core"), (2, 2, "xl"), (1, 6, "zp"), "bl0", (1, 5, "core"),
+    (1, 8, "core"), (2, 8, "core"), (2, 3, "core"), (2, 4, "core"), "bl1", (1, 10, "core"), (2, 4, "zp"), "wHc",
+    (2, 3, "zm"), (1, 13, "core"), (2, 6, "core"), (1, 12, "core"), "basm", (2, 5, "zm"), (2, 6, "xl"),
+    (1, 11, "core"), "wincot", (1, 3, "core"), (1, 14, "core"), (2, 9, "core"), (2, 10, "core"), "wHm",
+    (2, 5, "core"), (2, 11, "core"), "winmer", (2, 13, "core"), (2, 14, "core"), "fin1", (2, 12, "core"), "qkv",
+    "fin2", "up",
 ]
 
 TC, TL, BR, BL, BLX = 0, 1, 2, 3, 4
@@ -217,6 +218,55 @@
     return jnp.where(s < 80, tc, jnp.where(s < 128, tl, jnp.where(s < 176, br, bl)))
 
 
+def corner_split(t):
+    c = (t >= 144).astype(jnp.int32) + (t >= 288) + (t >= 432)
+    u = t - 144 * c
+    q = (u >= 36).astype(jnp.int32) + (u >= 72) + (u >= 108)
+    return 80 + 48 * c + u - 36 * q, q
+
+
+def to_corner(slot, q):
+    c = (slot >= 128).astype(jnp.int32) + (slot >= 176) + (slot >= 224)
+    return jnp.where(slot >= 80, 96 * c + slot - 80 + 36 * q, -1)
+
+
+def to_centre(slot, h):
+    return jnp.where((slot >= 0) & (slot < 80), slot + 72 * h, -1)
+
+
+def home_picks(t, u, shape):
+    slot, q = corner_split(t)
+    corner = slot_source(slot)
+    h = (u >= 72).astype(jnp.int32)
+    centre = slot_source(u - 72 * h)
+    corners = [pick(jnp.where(q == i, corner, -1), *shape(432)) for i in range(4)]
+    centres = [pick(jnp.where(h == i, centre, -1), *shape(144)) for i in range(2)]
+    return corners, centres
+
+
+def packed(picks, cells):
+    width = 1024 // len(picks)
+    parts = [dot(p, cells[:, width * i : width * i + width]) for i, p in enumerate(picks)]
+    return sum(parts[1:], parts[0]).astype(BF16)
+
+
+def unpacked(dst, rows, cells, corners, corner, centres, centre):
+    for i in range(4):
+        at = slice(256 * i, 256 * i + 256)
+        half = slice(256 * (i % 2), 256 * (i % 2) + 256)
+        total = dot(rows, cells[:, at]) + dot(corners[i], corner[...])
+        dst[:, at] = (total + dot(centres[i // 2], centre[:, half])).astype(BF16)
+
+
+def part_of(bufs, slot):
+    if len(bufs) == 1:
+        first, n = SLOT[slot]
+        return bufs[0].at[pl.ds(first, n)]
+    if slot == TC:
+        return bufs[1].at[pl.ds(0, 144)]
+    return bufs[0].at[pl.ds(144 * (slot - 1), 144)]
+
+
 def column(n):
     return lax.broadcasted_iota(jnp.int32, (n, 1), 0)
 
@@ -273,14 +323,24 @@
     f_recv,
     b_send,
     b_recv,
-    out_cot,
-    out_mer,
-    in_cot,
-    in_mer,
-    back_out,
-    back_grad,
-    home_out,
-    home_grad,
+    out_tag,
+    in_tag,
+    out_cot_c,
+    out_cot_t,
+    out_mer_c,
+    out_mer_t,
+    in_cot_c,
+    in_cot_t,
+    in_mer_c,
+    in_mer_t,
+    back_out_c,
+    back_out_t,
+    back_grad_c,
+    back_grad_t,
+    home_out_c,
+    home_out_t,
+    home_grad_c,
+    home_grad_t,
     patch_n,
     patch_f,
     patch_inv,
@@ -343,7 +403,11 @@
             if name in loads:
                 loads.pop(name).wait()
 
-    for ref in (in_cot, in_mer, home_out, home_grad):
+    out_cot, out_mer = (out_cot_c, out_cot_t), (out_mer_c, out_mer_t)
+    in_cot, in_mer = (in_cot_c, in_cot_t), (in_mer_c, in_mer_t)
+    back_out, back_grad = (back_out_c, back_out_t), (back_grad_c, back_grad_t)
+    home_out, home_grad = (home_out_c, home_out_t), (home_grad_c, home_grad_t)
+    for ref in (in_tag,) + in_cot + in_mer + home_out + home_grad:
         ref[...] = jnp.zeros_like(ref)
     barrier = pltpu.get_barrier_semaphore()
     partners = list(gather.near.values()) + [up, down, left, right, down_left, up_right]
@@ -355,12 +419,10 @@
 
     def forward(m, src, dst, do):
         def go(slot_from, slot_to, dev):
-            f0, n = SLOT[slot_from]
-            t0 = SLOT[slot_to][0]
             do(
                 pltpu.make_async_remote_copy(
-                    src_ref=src.at[pl.ds(f0, n)],
-                    dst_ref=dst.at[pl.ds(t0, n)],
+                    src_ref=part_of(src, slot_from),
+                    dst_ref=part_of(dst, slot_to),
                     send_sem=f_send.at[m, slot_from],
                     recv_sem=f_recv.at[m, slot_to],
                     device_id=dev,
@@ -385,8 +447,7 @@
 
     def forward_recv(m, dst):
         def got(slot):
-            f0, n = SLOT[slot]
-            part = dst.at[pl.ds(f0, n)]
+            part = part_of(dst, slot)
             pltpu.make_async_remote_copy(
                 src_ref=part,
                 dst_ref=part,
@@ -413,12 +474,10 @@
 
     def backward(m, w, src, dst, do):
         def go(slot_from, slot_to, dev):
-            f0, n = SLOT[slot_from]
-            t0 = SLOT[slot_to][0]
             do(
                 pltpu.make_async_remote_copy(
-                    src_ref=src.at[pl.ds(f0, n)],
-                    dst_ref=dst.at[pl.ds(t0, n)],
+                    src_ref=part_of(src, slot_from),
+                    dst_ref=part_of(dst, slot_to),
                     send_sem=b_send.at[m, slot_from],
                     recv_sem=b_recv.at[m, slot_to],
                     device_id=dev,
@@ -446,8 +505,7 @@
 
     def backward_recv(m, dst):
         def got(slot):
-            f0, n = SLOT[slot]
-            part = dst.at[pl.ds(f0, n)]
+            part = part_of(dst, slot)
             pltpu.make_async_remote_copy(
                 src_ref=part,
                 dst_ref=part,
@@ -490,11 +548,14 @@
         held_rows = jnp.sum(jnp.where(line(16) == lat, counts[...], 0), axis=-1, keepdims=True)
         tag = tag * (cell_row < held_rows).astype(F32)
         v["tag_home"] = jnp.broadcast_to(tag, (288, 128)).astype(BF16)
-        v["to_slots"] = pick(slot_source(column(OUT_ROWS)), OUT_ROWS, 288)
-        out_cot[:, 0:1024] = dot(v["to_slots"], cot[...]).astype(BF16)
-        out_cot[:, 1024:1152] = dot(v["to_slots"], v["tag_home"]).astype(BF16)
+        to_slots = pick(slot_source(column(OUT_ROWS)), OUT_ROWS, 288)
+        out_tag[...] = dot(to_slots, v["tag_home"]).astype(BF16)
+        v["out"] = home_picks(column(432), column(144), lambda n: (n, 288))
+        out_cot_c[...] = packed(v["out"][0], cot)
+        out_cot_t[...] = packed(v["out"][1], cot)
 
     def step_send_cot():
+        forward(2, (out_tag,), (in_tag,), start)
         forward(0, out_cot, in_cot, start)
 
     o = column(192)
@@ -559,19 +620,22 @@
             return 0
 
         lax.fori_loop(0, 2, merge_tile, 0)
-        out_mer[...] = dot(v["to_slots"], merged_home[...]).astype(BF16)
+        out_mer_c[...] = packed(v["out"][0], merged_home)
+        out_mer_t[...] = packed(v["out"][1], merged_home)
 
     def step_send_merged():
         forward(1, out_mer, in_mer, start)
 
     def owner():
         own, came = window_source(column(288), lat)
-        return pick(own, 288, 288), pick(came, 288, IN_ROWS)
+        corners = [pick(to_corner(came, i), 288, 576) for i in range(4)]
+        centres = [pick(to_centre(came, i), 288, 144) for i in range(2)]
+        return pick(own, 288, 288), corners, centres, pick(came, 288, IN_ROWS)
 
     def step_window_cot():
-        from_home, from_slots = owner()
-        win_cot[...] = (dot(from_home, cot[...]) + dot(from_slots, in_cot[:, 0:1024])).astype(BF16)
-        win_tag = dot(from_home, v["tag_home"]) + dot(from_slots, in_cot[:, 1024:1152])
+        from_home, corners, centres, from_slots = owner()
+        unpacked(win_cot, from_home, cot, corners, in_cot_c, centres, in_cot_t)
+        win_tag = dot(from_home, v["tag_home"]) + dot(from_slots, in_tag[...])
         d = lax.broadcasted_iota(jnp.int32, (288, 128), 0)
         apart = ((lat == 15) & (d >= 72) & (d < 144)) | ((lat == 0) & (d >= 144) & (d < 216))
         alive = (win_tag > 0).astype(F32)
@@ -585,8 +649,8 @@
             mask[w] = jnp.where(allowed, 0.0, MASKED)
 
     def step_window_merged():
-        from_home, from_slots = owner()
-        win_mer[...] = (dot(from_home, merged_home[...]) + dot(from_slots, in_mer[...])).astype(BF16)
+        from_home, corners, centres, _ = owner()
+        unpacked(win_mer, from_home, merged_home, corners, in_mer_c, centres, in_mer_t)
 
         loaded("attn_gain")
 
@@ -623,7 +687,7 @@
         fin2=lambda: gather.fin(2),
         merge=step_merge,
         Hm=step_send_merged,
-        wHc=lambda: forward_recv(0, in_cot),
+        wHc=lambda: (forward_recv(2, (in_tag,)), forward_recv(0, in_cot)),
         wHm=lambda: forward_recv(1, in_mer),
         wincot=step_window_cot,
         winmer=step_window_merged,
@@ -697,20 +761,15 @@
 
         lax.fori_loop(0, 3, two, 0)
 
-    def slots_of(w):
+    def put_slots(w, bufs, cells):
         _, came = window_source(line(144) + 144 * w, lat)
+        corner, centre = bufs
         if w == 1:
-            return pick(jnp.where(came >= 0, came - SLOT[TL][0], came), 144, 144)
-        came = jnp.where(came >= SLOT[BLX][0], came - SLOT[BLX][0] + 80, came)
-        return pick(came, 128, 144)
-
-    def put_slots(w, dst, cells):
-        moved = dot(slots_of(w), cells).astype(BF16)
-        if w == 1:
-            dst[80:224] = moved
+            corner[0:432] = packed([pick(to_corner(came, i), 432, 144) for i in range(4)], cells)
         else:
-            dst[0:80] = moved[0:80]
-            dst[224:272] = moved[80:128]
+            last = [jnp.where(came >= SLOT[BLX][0], to_corner(came, i) - 432, -1) for i in range(4)]
+            corner[432:576] = packed([pick(x, 144, 144) for x in last], cells)
+            centre[...] = packed([pick(to_centre(came, i), 144, 144) for i in range(2)], cells)
 
     def window_tail(w):
         rows = window_rows(w)
@@ -748,11 +807,11 @@
 
     own_l, _ = window_source(line(288), lat)
     to_home = pick(own_l, 288, 288)
-    slots_home = pick(slot_source(line(OUT_ROWS)), 288, OUT_ROWS)
+    corners_home, centres_home = home_picks(line(432), line(144), lambda n: (288, n))
     backward_recv(0, home_out)
-    out[...] = (dot(to_home, normed[...]) + dot(slots_home, home_out[...])).astype(BF16)
+    unpacked(out, to_home, normed, corners_home, home_out_c, centres_home, home_out_t)
     backward_recv(1, home_grad)
-    merged_home[...] = (dot(to_home, win_cot[...]) + dot(slots_home, home_grad[...])).astype(BF16)
+    unpacked(merged_home, to_home, win_cot, corners_home, home_grad_c, centres_home, home_grad_t)
 
     def patch_tile(n, _):
         at = pl.ds(pl.multiple_of(n * 1024, 1024), 1024)
@@ -781,6 +840,7 @@
     lax.fori_loop(0, 6, patch_back, 0)
 
     gather.drain()
+    forward(2, (out_tag,), (in_tag,), sent)
     forward(0, out_cot, in_cot, sent)
     forward(1, out_mer, in_mer, sent)
     for w in range(2):
@@ -811,18 +871,28 @@
             dma((3, N_IDS)),
             dma((3, N_IDS)),
             dma((3,)),
+            dma((3, 5)),
+            dma((3, 5)),
             dma((2, 5)),
             dma((2, 5)),
-            dma((2, 5)),
-            dma((2, 5)),
-            held(OUT_ROWS, 1152),
-            held(OUT_ROWS, 1024),
-            held(IN_ROWS, 1152),
-            held(IN_ROWS, 1024),
-            held(IN_ROWS, 1024),
-            held(IN_ROWS, 1024),
-            held(OUT_ROWS, 1024),
-            held(OUT_ROWS, 1024),
+            held(OUT_ROWS, 128),
+            held(IN_ROWS, 128),
+            held(432, 256),
+            held(144, 512),
+            held(432, 256),
+            held(144, 512),
+            held(576, 256),
+            held(144, 512),
+            held(576, 256),
+            held(144, 512),
+            held(576, 256),
+            held(144, 512),
+            held(576, 256),
+            held(144, 512),
+            held(432, 256),
+            held(144, 512),
+            held(432, 256),
+            held(144, 512),
             held(288, 2048),
             held(288, 2048, dtype=F32),
             held(288, 128, dtype=F32),

time: 80 us -> 77.8 us (0.972)
  Pallas kernels: 77.5 us -> 75.2 us
    pallas_call x1, Pallas kernels: 77.5 us -> 75.2 us  [local(): pl.pallas_call(kernel, out_shape=[pltpu.VMEM((288, 1024), BF16), pltpu.VM...]
where the time goes in v2:
time: 77.8 us; the launch traced here: 77.7 us
  Pallas kernels  75.2 us (97%)
  local copies, waits for them, and re-layouts  1.83 us (2%)
    pallas_call x1, Pallas kernels, local(): pl.pallas_call(kernel, out_shape=[pltpu.VMEM((288, 1024), BF16), pltpu.VM...  75.2 us
    unnamed x2, local copies, waits for them, and re-layouts  1.83 us

profile of v2, /device:TPU:6, one launch (start us, length us, event | category | flops | bytes accessed | tf_op | source)
XLA Modules:
  0.0 77.7 jit_solution(10532590382566782516)
XLA Ops:
  0.6 75.2 %shard_map.113 = (bf16[288,1024]{1,0:T(8,128)(2,1)S(1)}, bf16[1152,512]{1,0:T(8,128)(2,1)S(1)}) custom-call(bf16[1152,512]{1,0:T(8,128)(2,1)} %bitcast.9, f32[1,2048]{1,0:T(1,128)} %bitcast.11, bf16[128,1024]{1,0:T(8,128)(2,1)} %merge_shard.1, f32[1,1024]{1,0:T(1,128)} %bitcast.12, bf16[64,3072]{1,0:T(8,128)(2,1)} %qkv_shard.1, bf16[64,1024]{1,0:T(8,128)(2,1)} %proj_shard.1, ...), custom_call_target="tpu_custom_call" | custom-call | flops 10000000000 | bytes 20000000 | tf_op jit(solution)/shard_map/pallas_call | solution.py:859
  75.9 0.8 %copy.14 = bf16[12,24,1024]{2,1,0:T(8,128)(2,1)} copy(bf16[12,24,1024]{2,1,0:T(8,128)(2,1)S(1)} %bitcast.8) | data formatting | bytes 1179648
  76.7 1.0 %copy.15 = bf16[24,48,512]{2,1,0:T(8,128)(2,1)} copy(bf16[24,48,512]{2,1,0:T(8,128)(2,1)S(1)} %bitcast.7) | data formatting | bytes 2359296
